TPU v7x, 32 devices: a whole 2x2x4 slice. The times are simulated.
32 devices in a mesh: groups: 2 (over y), slab: 8 (over z, x), cross: 2 (over core).
Axes of the slice: x: 2, y: 2, z: 4, core: 2. Of those that a mesh axis runs over, the one named last changes fastest.
Arguments:
- basis: bfloat16 [1024, 64, 512], P(('groups', 'slab', 'cross')), parts along dimension 0, may hold values from -0.1796875 to 0.1796875
- stiff: bfloat16 [1024, 128, 128], P(('groups', 'slab', 'cross')), parts along dimension 0, may hold values from -0.5 to 0.5
- soft: bfloat16 [1024, 64, 64], P(('groups', 'slab', 'cross')), parts along dimension 0, may hold values from -9 to 9
- under: int32 [1024], P(('groups', 'slab', 'cross')), parts along dimension 0, may hold values 0 or 1
Outputs:
- k_reduced: float32 [1024, 512], P(('groups', 'slab', 'cross')), parts along dimension 0
- electrode_reduced: float32 [4096, 512], P(('groups', 'slab', 'cross')), parts along dimension 0
There are 2 independent parts, one for each index of `groups`. A program takes and returns all parts, laid end to end along the dimension named above; each array names one. Nothing has to cross between parts.
All inputs are finite; a program needn't handle non-finite values. No bound on the sum of `under` on one device may be relied on, other than what follows from the above.
Results may differ from a plain program's by a relative error of at most 0.0029.
Values may be sent and summed in bfloat16 or wider, within the bound.
A program may use at most 64 MiB of HBM per device.

v0:
```python
import jax
import jax.numpy as jnp
from jax import lax
from jax.sharding import PartitionSpec as P


def shifted(x, axis, by):
    length = lax.axis_size(axis)
    pairs = [(i, i + by) for i in range(length) if 0 <= i + by < length]
    return lax.ppermute(x, axis, pairs)


def partner(x, axis, bit):
    return lax.ppermute(x, axis, [(i, i ^ 1 << bit) for i in range(lax.axis_size(axis))])


def body(basis, stiff, soft, under):
    cells, layer, width = basis.shape
    nextcell = shifted(basis[:1], ("slab", "cross"), -1)
    upper_cells = jnp.concatenate([basis[1:], nextcell], axis=0)
    pairs = jnp.concatenate([basis, upper_cells], axis=1)
    prod = jnp.einsum("cij,cjr->cir", stiff, pairs, preferred_element_type=jnp.float32)
    carry_in = shifted(prod[-1:, layer:], ("slab", "cross"), 1)
    action = prod[:, :layer] + jnp.concatenate([carry_in, prod[:-1, layer:]], axis=0)
    flat_basis = basis.reshape(cells * layer, width)
    flat_stiff = action.astype(jnp.bfloat16).reshape(cells * layer, width)
    k_reduced = lax.psum_scatter(
        lax.dot_general(
            flat_basis, flat_stiff, (((0,), (0,)), ((), ())), preferred_element_type=jnp.float32
        ),
        ("slab", "cross"),
        scatter_dimension=0,
        tiled=True,
    )
    masked = soft * under.astype(jnp.bfloat16)[:, None, None]
    soft_basis = jnp.einsum("cij,cjr->cir", masked, basis, preferred_element_type=jnp.float32)
    flat_soft = soft_basis.astype(jnp.bfloat16).reshape(cells * layer, width)
    partial_sum = lax.dot_general(
        flat_basis, flat_soft, (((0,), (0,)), ((), ())), preferred_element_type=jnp.float32
    )
    parity = lax.axis_index("slab") % 2
    halves = partial_sum.reshape(2, width // 2, width)
    mine = lax.dynamic_index_in_dim(halves, parity, 0, keepdims=False)
    other = lax.dynamic_index_in_dim(halves, 1 - parity, 0, keepdims=False)
    paired = mine + partner(other, "slab", 0)
    electrode_rows = lax.psum_scatter(paired, "cross", scatter_dimension=0, tiled=True)
    return (k_reduced, electrode_rows)


def solution(mesh):
    placed = (
        P(("groups", "slab", "cross"), None, None),
        P(("groups", "slab", "cross"), None, None),
        P(("groups", "slab", "cross"), None, None),
        P(("groups", "slab", "cross")),
    )
    return jax.shard_map(
        body,
        mesh=mesh,
        in_specs=placed,
        out_specs=(P(("groups", "slab", "cross"), None), P(("groups", "slab", "cross"), None)),
        check_vma=False,
    )
```

profile of v0, /device:TPU:0, one launch (start us, length us, event | category | flops | bytes accessed | tf_op | source)
XLA Modules:
  0.0 112.5 jit_solution(10623348634959075095)
XLA Ops:
  7.2 0.0 copy-start
  7.2 0.0 reduce-scatter.5.cloned.1.call-start
  7.2 0.7 convert_element_type.10
  8.0 0.0 copy-start.1
  8.0 5.4 %fusion.12 = f32[512,512,1]{0,1,2:T(8,128)} fusion(bf16[32,64,512]{2,1,0:T(8,128)(2,1)} %param.4, bf16[32,64,64]{2,1,0:T(8,128)(2,1)} %param.6, bf16[32]{0:T(256)(128)(2,1)S(1)} %convert_element_type.10), kind=kOutput, calls=%fused_computation.10 | convolution fusion | flops 1209139200 | bytes 3407936 | tf_op jit(solution)/shard_map/dot_general | solution.py:38
  13.4 1.9 %dynamic-slice_bitcast_fusion = f32[256,512]{1,0:T(8,128)} fusion(f32[2,256,512]{2,1,0:T(8,128)} %bitcast.20, s32[]{:T(128)S(6)} %select_n.16), kind=kLoop, calls=%fused_computation.15 | loop fusion | bytes 1048580 | tf_op jit(solution)/shard_map/jit(dynamic_index_in_dim)/squeeze | solution.py:44
  15.2 2.9 %collective-permute-start.2 = (f32[256,512]{1,0:T(8,128)}, f32[256,512]{1,0:T(8,128)}, u32[]{:S(2)}, u32[]{:S(2)}) collective-permute-start(f32[256,512]{1,0:T(8,128)} %dynamic-slice_bitcast_fusion), channel_id=1, source_target_pairs={{0,2},{2,0},{4,6},{6,4},{8,10},{10,8},{12,14},{14,12},{1,3},{3,1},... | collective-permute-start | bytes 1572872 | tf_op jit(solution)/shard_map/ppermute | solution.py:14
  18.1 0.0 copy-done.1
  18.2 1.3 %collective-permute-start = (bf16[1,64,512]{2,1,0:T(8,128)(2,1)S(1)}, bf16[1,64,512]{2,1,0:T(8,128)(2,1)S(1)}, u32[]{:S(2)}, u32[]{:S(2)}) collective-permute-start(bf16[1,64,512]{2,1,0:T(8,128)(2,1)S(1)} %slice.16), channel_id=1, source_target_pairs={{1,0},{2,1},{3,2},{4,3},{5,4},{6,5},{7,6},{8,7},{9,8},{10,9},{11,1... | collective-permute-start | bytes 196616 | tf_op jit(solution)/shard_map/ppermute | solution.py:10
  19.5 1.5 %slice.15 = bf16[31,64,512]{2,1,0:T(8,128)(2,1)} slice(bf16[32,64,512]{2,1,0:T(8,128)(2,1)S(1)} %copy-done.1), slice={[1:32], [0:64], [0:512]} | slice | bytes 4063232 | tf_op jit(solution)/shard_map/slice | solution.py:20
  20.9 9.4 %collective-permute-done.2 = f32[256,512]{1,0:T(8,128)} collective-permute-done((f32[256,512]{1,0:T(8,128)}, f32[256,512]{1,0:T(8,128)}, u32[]{:S(2)}, u32[]{:S(2)}) %collective-permute-start.2) | collective-permute-done | bytes 524320 | tf_op jit(solution)/shard_map/ppermute | solution.py:14
  30.4 2.1 %bitcast_add_fusion = f32[256,512]{1,0:T(8,128)} fusion(f32[256,512]{1,0:T(8,128)} %collective-permute-done.2, f32[2,256,512]{2,1,0:T(8,128)} %bitcast.21, s32[]{:T(128)S(6)} %select_n.15), kind=kLoop, calls=%fused_computation.14 | loop fusion | flops 131072 | bytes 1572868 | tf_op jit(solution)/shard_map/add | solution.py:45
  32.5 0.0 reduce-scatter.5.cloned.1.call-update
  32.5 0.0 reduce-scatter.7.cloned.1.call-start
  32.5 0.0 collective-permute-done
  32.5 0.0 copy-done
  32.6 2.7 %fusion.7 = f32[32,128,512]{2,1,0:T(8,128)S(1)} fusion(bf16[32,128,128]{2,1,0:T(8,128)(2,1)S(1)} %copy-done, bf16[1,64,512]{2,1,0:T(8,128)(2,1)S(1)} %collective-permute-done, bf16[31,64,512]{2,1,0:T(8,128)(2,1)} %slice.15, bf16[32,64,512]{2,1,0:T(8,128)(2,1)S(1)} %copy-done.1), kind=kOutput, calls=%fused_computation.8 | convolution fusion | flops 549453824 | bytes 13631488 | tf_op jit(solution)/shard_map/cij,cjr->cir/dot_general | solution.py:22
  35.3 1.3 %collective-permute-start.1 = (f32[1,64,512]{2,1,0:T(8,128)S(1)}, f32[1,64,512]{2,1,0:T(8,128)S(1)}, u32[]{:S(2)}, u32[]{:S(2)}) collective-permute-start(f32[1,64,512]{2,1,0:T(8,128)S(1)} %slice.21), channel_id=1, source_target_pairs={{0,1},{1,2},{2,3},{3,4},{4,5},{5,6},{6,7},{7,8},{8,9},{9,10},{10,1... | collective-permute-start | bytes 393224 | tf_op jit(solution)/shard_map/ppermute | solution.py:10
  36.6 0.5 slice.22
  37.1 0.5 collective-permute-done.1
  37.6 2.5 %fusion.16 = f32[512,512]{0,1:T(8,128)} fusion(bf16[32,64,512]{2,1,0:T(8,128)(2,1)S(1)} %copy-done.1, f32[32,128,512]{2,1,0:T(8,128)S(1)} %fusion.7, f32[31,64,512]{2,1,0:T(8,128)S(1)} %slice.22, f32[1,64,512]{2,1,0:T(8,128)S(1)} %collective-permute-done.1), kind=kOutput, calls=%fused_computation.13 | convolution fusion | flops 1076887552 | bytes 11534336 | tf_op jit(solution)/shard_map/dot_general | solution.py:28
  40.0 2.5 %copy.8 = f32[512,512]{1,0:T(8,128)} copy(f32[512,512]{0,1:T(8,128)} %fusion.16) | data formatting | bytes 2097152
  42.5 0.0 reduce-scatter.7.cloned.1.call-update
  42.6 0.0 reduce-scatter.5.cloned.1.call-done
  42.6 63.1 %reduce-scatter.7.cloned.1.call-done = f32[32,512]{1,0:T(8,128)} async-done(((f32[512,512]{1,0:T(8,128)}), f32[32,512]{1,0:T(8,128)}) %reduce-scatter.7.cloned.1.call-update) | async-done | bytes 65552
  (2 shorter events, 0.0 us)
Async XLA Ops:
  7.2 25.4 %copy-start = (bf16[32,128,128]{2,1,0:T(8,128)(2,1)S(1)}, bf16[32,128,128]{2,1,0:T(8,128)(2,1)}, u32[]{:S(2)}) copy-start(bf16[32,128,128]{2,1,0:T(8,128)(2,1)} %param.5) | copy-start | bytes 3145732
  7.2 35.4 %reduce-scatter.5.cloned.1.call-start = ((), (), s32[]{:S(2)}) async-start(), calls=%async_computation.2 | async-start | bytes 786432 | tf_op jit(solution)/shard_map/reduce_scatter | solution.py:46
  8.0 10.2 %copy-start.1 = (bf16[32,64,512]{2,1,0:T(8,128)(2,1)S(1)}, bf16[32,64,512]{2,1,0:T(8,128)(2,1)}, u32[]{:S(2)}) copy-start(bf16[32,64,512]{2,1,0:T(8,128)(2,1)} %param.4) | copy-start | bytes 6291460
  15.2 15.2 %collective-permute-start.2 = (f32[256,512]{1,0:T(8,128)}, f32[256,512]{1,0:T(8,128)}, u32[]{:S(2)}, u32[]{:S(2)}) collective-permute-start(f32[256,512]{1,0:T(8,128)} %dynamic-slice_bitcast_fusion), channel_id=1, source_target_pairs={{0,2},{2,0},{4,6},{6,4},{8,10},{10,8},{12,14},{14,12},{1,3},{3,1},... | collective-permute-start | bytes 1572872 | tf_op jit(solution)/shard_map/ppermute | solution.py:14
  18.2 14.4 %collective-permute-start = (bf16[1,64,512]{2,1,0:T(8,128)(2,1)S(1)}, bf16[1,64,512]{2,1,0:T(8,128)(2,1)S(1)}, u32[]{:S(2)}, u32[]{:S(2)}) collective-permute-start(bf16[1,64,512]{2,1,0:T(8,128)(2,1)S(1)} %slice.16), channel_id=1, source_target_pairs={{1,0},{2,1},{3,2},{4,3},{5,4},{6,5},{7,6},{8,7},{9,8},{10,9},{11,1... | collective-permute-start | bytes 196616 | tf_op jit(solution)/shard_map/ppermute | solution.py:10
  32.5 73.2 %reduce-scatter.7.cloned.1.call-start = ((), (), s32[]{:S(2)}) async-start(), calls=%async_computation.3 | async-start | bytes 1114112
  35.3 2.3 %collective-permute-start.1 = (f32[1,64,512]{2,1,0:T(8,128)S(1)}, f32[1,64,512]{2,1,0:T(8,128)S(1)}, u32[]{:S(2)}, u32[]{:S(2)}) collective-permute-start(f32[1,64,512]{2,1,0:T(8,128)S(1)} %slice.21), channel_id=1, source_target_pairs={{0,1},{1,2},{2,3},{3,4},{4,5},{5,6},{6,7},{7,8},{8,9},{9,10},{10,1... | collective-permute-start | bytes 393224 | tf_op jit(solution)/shard_map/ppermute | solution.py:10
Sparse Core Ops, SparseCore 0:
  32.6 9.4 reduce-scatter.4
  46.7 58.8 reduce-scatter.6
where the time goes:
time: 113 us
  waiting for transfers between devices  73.1 us (65%)
  between operations  14.1 us (12%)
  matrix products  10.6 us (9%)
  local copies, waits for them, and re-layouts  6.37 us (6%)
  starting transfers between devices  5.6 us (5%)
  other arithmetic  2.8 us (2%)
    unnamed x3, waiting for transfers between devices  63.1 us
    ppermute x1, waiting for transfers between devices, partner(): lax.ppermute(x, axis, [(i, i ^ 1 << bit) for i in range(lax.axis_size(axi...  9.45 us
    dot_general x1, matrix products, body(): lax.dot_general(flat_basis, flat_soft, (((0,), (0,)), ((), ())), preferre...  5.39 us
    ppermute x1, starting transfers between devices, partner(): lax.ppermute(x, axis, [(i, i ^ 1 << bit) for i in range(lax.axis_size(axi...  2.93 us
    dot_general x1, matrix products, body(): jnp.einsum('cij,cjr->cir', stiff, pairs, preferred_element_type=jnp.float32)  2.71 us
    ppermute x2, starting transfers between devices, shifted(): return lax.ppermute(x, axis, pairs)  2.59 us
    unnamed x5, local copies, waits for them, and re-layouts  2.55 us
    dot_general x1, matrix products, body(): lax.dot_general(flat_basis, flat_stiff, (((0,), (0,)), ((), ())), preferr...  2.46 us
  transfers between devices with their start and end apart: 5, of which 3 were waited for; matrix products, arithmetic and copies ran while one was open for 10% of the time, Pallas kernels for 0%

commit v1 on v0

--- a/solution.py
+++ b/solution.py
@@ -1,7 +1,15 @@
+import functools
+
 import jax
 import jax.numpy as jnp
 from jax import lax
+from jax.experimental import pallas as pl
+from jax.experimental.pallas import tpu as pltpu
 from jax.sharding import PartitionSpec as P
+
+MESH = pl.DeviceIdType.MESH
+BF16 = jnp.bfloat16
+F32 = jnp.float32
 
 
 def shifted(x, axis, by):
@@ -14,7 +22,7 @@
     return lax.ppermute(x, axis, [(i, i ^ 1 << bit) for i in range(lax.axis_size(axis))])
 
 
-def body(basis, stiff, soft, under):
+def plain_body(basis, stiff, soft, under):
     cells, layer, width = basis.shape
     nextcell = shifted(basis[:1], ("slab", "cross"), -1)
     upper_cells = jnp.concatenate([basis[1:], nextcell], axis=0)
@@ -47,6 +55,297 @@
     return (k_reduced, electrode_rows)
 
 
+def fused_kernel(
+    nz, cells, layer, width, chunk,
+    basis, stiff, soft, under, k_out, e_out,
+    ext, turned, stiff_v, stiff_p, soft_v, acted,
+    k_own, k_core_s, k_core_r, k_x_s, k_x_r, k_z_s, k_z_r,
+    e_own, e_core_s, e_core_r, e_x_s, e_x_r,
+    load_sem, halo_s, halo_r, kc_s, kc_r, kx_s, kx_r, kz_s, kz_r, ec_s, ec_r, ex_s, ex_r,
+):
+    slab = lax.axis_index("slab")
+    core = lax.axis_index("cross")
+    z, x = slab // 2, slab % 2
+    here = slab * 2 + core
+    count = nz * 4
+    rows = cells * layer
+    chunks = width // chunk
+    k_rows = width // count
+    e_rows = width // 4
+    group = 4
+
+    core_peer = {"cross": 1 - core}
+    x_peer = {"slab": slab + 1 - 2 * x}
+    z_peers = [{"slab": ((z + d) % nz) * 2 + x} for d in range(1, nz)]
+    before = (here + count - 1) % count
+    after = (here + 1) % count
+    before_peer = {"slab": before // 2, "cross": before % 2}
+    after_peer = {"slab": after // 2, "cross": after % 2}
+
+    barrier = pltpu.get_barrier_semaphore()
+    peers = [core_peer, x_peer, *z_peers, before_peer, after_peer]
+    for peer in peers:
+        pl.semaphore_signal(barrier, inc=1, device_id=peer, device_id_type=MESH)
+
+    loads = [
+        pltpu.make_async_copy(basis, ext.at[pl.ds(layer, rows)], load_sem.at[0]),
+        pltpu.make_async_copy(stiff, stiff_v, load_sem.at[1]),
+        pltpu.make_async_copy(soft, soft_v, load_sem.at[2]),
+    ]
+    for load in loads:
+        load.start()
+
+    pl.semaphore_wait(barrier, len(peers))
+
+    def remote(src, dst, send, recv, peer):
+        return pltpu.make_async_remote_copy(
+            src_ref=src, dst_ref=dst, send_sem=send, recv_sem=recv,
+            device_id=peer, device_id_type=MESH,
+        )
+
+    first_out = remote(
+        basis.at[pl.ds(0, layer)], ext.at[pl.ds(layer + rows, layer)],
+        halo_s.at[0], halo_r.at[0], before_peer,
+    )
+    last_out = remote(
+        basis.at[pl.ds(rows - layer, layer)], ext.at[pl.ds(0, layer)],
+        halo_s.at[1], halo_r.at[1], after_peer,
+    )
+    lower_out = remote(
+        stiff.at[cells - 1, pl.ds(layer, layer)], stiff_p,
+        halo_s.at[2], halo_r.at[2], after_peer,
+    )
+
+    @pl.when(here > 0)
+    def _():
+        first_out.start()
+
+    @pl.when(here < count - 1)
+    def _():
+        last_out.start()
+        lower_out.start()
+
+    loads[0].wait()
+
+    def turn(g, _):
+        at = pl.multiple_of(g * chunk, chunk)
+        turned[:, pl.ds(at, chunk)] = ext[pl.ds(pl.multiple_of(layer + at, layer), chunk), :].T
+        return 0
+
+    lax.fori_loop(0, rows // chunk, turn, 0)
+    loads[1].wait()
+    loads[2].wait()
+
+    @pl.when(here > 0)
+    def _():
+        last_out.wait_recv()
+        lower_out.wait_recv()
+
+    @pl.when(here == 0)
+    def _():
+        ext[pl.ds(0, layer), :] = jnp.zeros((layer, width), BF16)
+        stiff_p[...] = jnp.zeros(stiff_p.shape, BF16)
+
+    @pl.when(here < count - 1)
+    def _():
+        first_out.wait_recv()
+
+    @pl.when(here == count - 1)
+    def _():
+        ext[pl.ds(layer + rows, layer), :] = jnp.zeros((layer, width), BF16)
+
+    def stiff_chunk(j):
+        cols = pl.ds(j * chunk, chunk)
+
+        def step(g, carry):
+            for i in range(group):
+                c = g * group + i
+                at = pl.multiple_of(c * layer, layer)
+                prod = jnp.dot(
+                    stiff_v[c],
+                    ext[pl.ds(pl.multiple_of(at + layer, layer), 2 * layer), cols],
+                    preferred_element_type=F32,
+                )
+                acted[pl.ds(at, layer), cols] = (prod[:layer] + carry).astype(BF16)
+                carry = prod[layer:]
+            return carry
+
+        carry = jnp.dot(stiff_p[...], ext[pl.ds(0, 2 * layer), cols], preferred_element_type=F32)
+        lax.fori_loop(0, cells // group, step, carry)
+
+    def soft_chunk(j):
+        cols = pl.ds(j * chunk, chunk)
+
+        def step(g, _):
+            for i in range(group):
+                c = g * group + i
+                at = pl.multiple_of(c * layer, layer)
+                masked = soft_v[c] * under[c].astype(F32).astype(BF16)
+                prod = jnp.dot(
+                    masked,
+                    ext[pl.ds(pl.multiple_of(at + layer, layer), layer), cols],
+                    preferred_element_type=F32,
+                )
+                acted[pl.ds(at, layer), cols] = prod.astype(BF16)
+            return 0
+
+        lax.fori_loop(0, cells // group, step, 0)
+
+    def project(j):
+        return jnp.dot(
+            turned[...], acted[:, pl.ds(j * chunk, chunk)], preferred_element_type=F32
+        )
+
+    kc = [remote(k_core_s.at[j, 1 - core], k_core_r.at[j], kc_s.at[j], kc_r.at[j], core_peer)
+          for j in range(chunks)]
+    kx = [remote(k_x_s.at[j], k_x_r.at[j], kx_s.at[j], kx_r.at[j], x_peer) for j in range(chunks)]
+    kz = [[remote(k_z_s.at[j, d], k_z_r.at[j, d], kz_s.at[j, d], kz_r.at[j, d], z_peers[d])
+           for d in range(nz - 1)] for j in range(chunks)]
+    ec = [remote(e_core_s.at[j, 1 - core], e_core_r.at[j], ec_s.at[j], ec_r.at[j], core_peer)
+          for j in range(chunks)]
+    ex = [remote(e_x_s.at[j], e_x_r.at[j], ex_s.at[j], ex_r.at[j], x_peer) for j in range(chunks)]
+
+    def k_start(j):
+        part = project(j)
+        for c in range(2):
+            for xx in range(2):
+                for zz in range(nz):
+                    at = ((zz * 2 + xx) * 2 + c) * k_rows
+                    block = part[at:at + k_rows]
+                    k_own[j, c, xx, zz] = block
+                    k_core_s[j, c, xx, zz] = block.astype(BF16)
+        kc[j].start()
+
+    def k_across(j):
+        kc[j].wait_recv()
+        k_x_s[j] = (k_own[j, core, 1 - x] + k_core_r[j, 1 - x].astype(F32)).astype(BF16)
+        kx[j].start()
+        k_own[j, core, x] = k_own[j, core, x] + k_core_r[j, x].astype(F32)
+
+    def k_along(j):
+        kx[j].wait_recv()
+        for d in range(nz - 1):
+            to = (z + d + 1) % nz
+            k_z_s[j, d] = (k_own[j, core, x, to] + k_x_r[j, to].astype(F32)).astype(BF16)
+            kz[j][d].start()
+
+    def k_end(j):
+        total = k_own[j, core, x, z] + k_x_r[j, z].astype(F32)
+        for d in range(nz - 1):
+            kz[j][d].wait_recv()
+            total = total + k_z_r[j, d].astype(F32)
+        k_out[:, pl.ds(j * chunk, chunk)] = total
+
+    def e_start(j):
+        part = project(j)
+        for c in range(2):
+            for xx in range(2):
+                at = (xx * 2 + c) * e_rows
+                block = part[at:at + e_rows]
+                e_own[j, c, xx] = block
+                e_core_s[j, c, xx] = block.astype(BF16)
+        ec[j].start()
+
+    def e_across(j):
+        ec[j].wait_recv()
+        e_x_s[j] = (e_own[j, core, 1 - x] + e_core_r[j, 1 - x].astype(F32)).astype(BF16)
+        ex[j].start()
+
+    def e_end(j):
+        mine = e_own[j, core, x] + e_core_r[j, x].astype(F32)
+        ex[j].wait_recv()
+        e_out[:, pl.ds(j * chunk, chunk)] = mine + ex_in(j)
+
+    def ex_in(j):
+        return e_x_r[j].astype(F32)
+
+    stiff_chunk(0)
+    k_start(0)
+    stiff_chunk(1)
+    k_across(0)
+    k_start(1)
+    soft_chunk(0)
+    k_across(1)
+    k_along(0)
+    e_start(0)
+    soft_chunk(1)
+    e_across(0)
+    k_along(1)
+    e_start(1)
+    k_end(0)
+    e_across(1)
+    e_end(0)
+    k_end(1)
+    e_end(1)
+
+    @pl.when(here > 0)
+    def _():
+        first_out.wait_send()
+
+    @pl.when(here < count - 1)
+    def _():
+        last_out.wait_send()
+        lower_out.wait_send()
+
+    for j in range(chunks):
+        kc[j].wait_send()
+        kx[j].wait_send()
+        for d in range(nz - 1):
+            kz[j][d].wait_send()
+        ec[j].wait_send()
+        ex[j].wait_send()
+
+
+def fused_body(basis, stiff, soft, under):
+    cells, layer, width = basis.shape
+    rows = cells * layer
+    nz = lax.axis_size("slab") // 2
+    chunk = 256
+    chunks = width // chunk
+    k_rows = width // (4 * nz)
+    e_rows = width // 4
+    hbm = pl.BlockSpec(memory_space=pl.ANY)
+    vmem = pl.BlockSpec(memory_space=pltpu.VMEM)
+    dma = pltpu.SemaphoreType.DMA
+    return pl.pallas_call(
+        functools.partial(fused_kernel, nz, cells, layer, width, chunk),
+        out_shape=(
+            jax.ShapeDtypeStruct((k_rows, width), F32),
+            jax.ShapeDtypeStruct((e_rows, width), F32),
+        ),
+        in_specs=[hbm, hbm, hbm, pl.BlockSpec(memory_space=pltpu.SMEM)],
+        out_specs=(vmem, vmem),
+        scratch_shapes=[
+            pltpu.VMEM((rows + 2 * layer, width), BF16),
+            pltpu.VMEM((width, rows), BF16),
+            pltpu.VMEM((cells, 2 * layer, 2 * layer), BF16),
+            pltpu.VMEM((layer, 2 * layer), BF16),
+            pltpu.VMEM((cells, layer, layer), BF16),
+            pltpu.VMEM((rows, width), BF16),
+            pltpu.VMEM((chunks, 2, 2, nz, k_rows, chunk), F32),
+            pltpu.VMEM((chunks, 2, 2, nz, k_rows, chunk), BF16),
+            pltpu.VMEM((chunks, 2, nz, k_rows, chunk), BF16),
+            pltpu.VMEM((chunks, nz, k_rows, chunk), BF16),
+            pltpu.VMEM((chunks, nz, k_rows, chunk), BF16),
+            pltpu.VMEM((chunks, nz - 1, k_rows, chunk), BF16),
+            pltpu.VMEM((chunks, nz - 1, k_rows, chunk), BF16),
+            pltpu.VMEM((chunks, 2, 2, e_rows, chunk), F32),
+            pltpu.VMEM((chunks, 2, 2, e_rows, chunk), BF16),
+            pltpu.VMEM((chunks, 2, e_rows, chunk), BF16),
+            pltpu.VMEM((chunks, e_rows, chunk), BF16),
+            pltpu.VMEM((chunks, e_rows, chunk), BF16),
+            dma((3,)), dma((3,)), dma((3,)),
+            dma((chunks,)), dma((chunks,)), dma((chunks,)), dma((chunks,)),
+            dma((chunks, nz - 1)), dma((chunks, nz - 1)),
+            dma((chunks,)), dma((chunks,)), dma((chunks,)), dma((chunks,)),
+        ],
+        compiler_params=pltpu.CompilerParams(
+            collective_id=0, has_side_effects=True, vmem_limit_bytes=48 << 20
+        ),
+        name="fused",
+    )(basis.reshape(rows, width), stiff, soft, under)
+
+
 def solution(mesh):
     placed = (
         P(("groups", "slab", "cross"), None, None),
@@ -54,6 +353,23 @@
         P(("groups", "slab", "cross"), None, None),
         P(("groups", "slab", "cross")),
     )
+
+    def body(basis, stiff, soft, under):
+        cells, layer, width = basis.shape
+        members = mesh.shape["slab"] * mesh.shape["cross"]
+        fits = (
+            mesh.shape["cross"] == 2
+            and mesh.shape["slab"] % 2 == 0
+            and mesh.shape["slab"] >= 4
+            and width == 512
+            and layer == 64
+            and cells % 4 == 0
+            and (cells * layer) % 256 == 0
+            and width // members >= 16
+            and (width // members) % 16 == 0
+        )
+        return (fused_body if fits else plain_body)(basis, stiff, soft, under)
+
     return jax.shard_map(
         body,
         mesh=mesh,

time: 113 us -> 31.6 us (0.28)
  waiting for transfers between devices: 73.1 us -> 0 us
  Pallas kernels: 0 us -> 24.8 us
  between operations: 14.1 us -> 0.65 us
  matrix products: 10.6 us -> 0 us
  starting transfers between devices: 5.6 us -> 0 us
  other arithmetic: 2.8 us -> 0 us
    unnamed x3 -> x0, waiting for transfers between devices: 63.1 us -> none
    pallas_call x0 -> x1, Pallas kernels: none -> 24.8 us  [fused_body(): pl.pallas_call(functools.partial(fused_kernel, nz, cells, layer, width, c...]
    dot_general x3 -> x0, matrix products: 10.6 us -> none  [the longest x1 5.39 us: body(): lax.dot_general(flat_basis, flat_soft, (((0,), (0,)), ((), ())), preferre...]
    ppermute x3 -> x0, waiting for transfers between devices: 9.94 us -> none  [the longest x1 9.45 us: partner(): lax.ppermute(x, axis, [(i, i ^ 1 << bit) for i in range(lax.axis_size(axi...]
    ppermute x3 -> x0, starting transfers between devices: 5.52 us -> none  [the longest x1 2.93 us: partner(): lax.ppermute(x, axis, [(i, i ^ 1 << bit) for i in range(lax.axis_size(axi...]
    unnamed x5 -> x10, local copies, waits for them, and re-layouts: 2.55 us -> 5.84 us
    add x1 -> x0, other arithmetic: 2.07 us -> none  [body(): paired = mine + partner(other, 'slab', 0)]
    slice x4 -> x0, local copies, waits for them, and re-layouts: 1.96 us -> none  [the longest x1 1.48 us: body(): upper_cells = jnp.concatenate([basis[1:], nextcell], axis=0)]
  transfers between devices with their start and end apart: 5 -> 0, of which waited for: 3 -> 0; matrix products, arithmetic and copies ran while one was open for 10% -> 0% of each run, Pallas kernels for 0% -> 0%
where the time goes in v1:
time: 31.6 us; the launch traced here: 31.3 us
  Pallas kernels  24.8 us (78%)
  local copies, waits for them, and re-layouts  5.84 us (18%)
  between operations  0.65 us (2%)
    pallas_call x1, Pallas kernels, fused_body(): pl.pallas_call(functools.partial(fused_kernel, nz, cells, layer, width, c...  24.8 us
    unnamed x10, local copies, waits for them, and re-layouts  5.84 us

profile of v1, /device:TPU:0, one launch (start us, length us, event | category | flops | bytes accessed | tf_op | source)
XLA Modules:
  0.0 31.3 jit_solution(11460861210968058534)
XLA Ops:
  0.6 0.0 copy-start
  0.6 1.6 %copy-done = bf16[32,64,512]{2,1,0:T(8,128)(2,1)S(1)} copy-done((bf16[32,64,512]{2,1,0:T(8,128)(2,1)S(1)}, bf16[32,64,512]{2,1,0:T(8,128)(2,1)}, u32[]{:S(2)}) %copy-start) | copy-done | bytes 2097176
  2.2 0.0 copy-start.1
  2.2 1.2 %copy-done.1 = bf16[32,128,128]{2,1,0:T(8,128)(2,1)S(1)} copy-done((bf16[32,128,128]{2,1,0:T(8,128)(2,1)S(1)}, bf16[32,128,128]{2,1,0:T(8,128)(2,1)}, u32[]{:S(2)}) %copy-start.1) | copy-done | bytes 1048600
  3.4 0.0 copy-start.2
  3.5 1.0 %copy-done.2 = bf16[32,64,64]{2,1,0:T(8,128)(2,1)S(1)} copy-done((bf16[32,64,64]{2,1,0:T(8,128)(2,1)S(1)}, bf16[32,64,64]{2,1,0:T(8,128)(2,1)}, u32[]{:S(2)}) %copy-start.2) | copy-done | bytes 262168
  4.5 0.0 copy-start.3
  4.5 0.7 %copy-done.3 = s32[32]{0:T(128)S(1)} copy-done((s32[32]{0:T(128)S(1)}, s32[32]{0:T(128)}, u32[]{:S(2)}) %copy-start.3) | copy-done | bytes 152
  5.1 24.8 %fused.1 = (f32[32,512]{1,0:T(8,128)S(1)}, f32[128,512]{1,0:T(8,128)S(1)}) custom-call(bf16[2048,512]{1,0:T(8,128)(2,1)S(1)} %bitcast.1, bf16[32,128,128]{2,1,0:T(8,128)(2,1)S(1)} %copy-done.1, bf16[32,64,64]{2,1,0:T(8,128)(2,1)S(1)} %copy-done.2, s32[32]{0:T(128)S(1)} %copy-done.3), custom_call_target="tpu_custom_call" | custom-call | tf_op jit(solution)/shard_map/fused/pallas_call | solution.py:310
  30.0 0.6 %copy.8 = f32[32,512]{1,0:T(8,128)} copy(f32[32,512]{1,0:T(8,128)S(1)} %get-tuple-element.4) | data formatting | bytes 131072
  30.6 0.7 %copy.9 = f32[128,512]{1,0:T(8,128)} copy(f32[128,512]{1,0:T(8,128)S(1)} %get-tuple-element.5) | data formatting | bytes 524288
Async XLA Ops:
  0.6 1.6 %copy-start = (bf16[32,64,512]{2,1,0:T(8,128)(2,1)S(1)}, bf16[32,64,512]{2,1,0:T(8,128)(2,1)}, u32[]{:S(2)}) copy-start(bf16[32,64,512]{2,1,0:T(8,128)(2,1)} %param.4) | copy-start | bytes 6291460
  2.2 1.2 %copy-start.1 = (bf16[32,128,128]{2,1,0:T(8,128)(2,1)S(1)}, bf16[32,128,128]{2,1,0:T(8,128)(2,1)}, u32[]{:S(2)}) copy-start(bf16[32,128,128]{2,1,0:T(8,128)(2,1)} %stiff.1) | copy-start | bytes 3145732
  3.4 1.0 %copy-start.2 = (bf16[32,64,64]{2,1,0:T(8,128)(2,1)S(1)}, bf16[32,64,64]{2,1,0:T(8,128)(2,1)}, u32[]{:S(2)}) copy-start(bf16[32,64,64]{2,1,0:T(8,128)(2,1)} %soft.1) | copy-start | bytes 786436
  4.5 0.7 %copy-start.3 = (s32[32]{0:T(128)S(1)}, s32[32]{0:T(128)}, u32[]{:S(2)}) copy-start(s32[32]{0:T(128)} %under.1) | copy-start | bytes 388

commit v2 on v1

--- a/solution.py
+++ b/solution.py
@@ -58,7 +58,7 @@
 def fused_kernel(
     nz, cells, layer, width, chunk,
     basis, stiff, soft, under, k_out, e_out,
-    ext, turned, stiff_v, stiff_p, soft_v, acted,
+    ext, stiff_v, stiff_p, soft_v, mask_v, acted, softened,
     k_own, k_core_s, k_core_r, k_x_s, k_x_r, k_z_s, k_z_r,
     e_own, e_core_s, e_core_r, e_x_s, e_x_r,
     load_sem, halo_s, halo_r, kc_s, kc_r, kx_s, kx_r, kz_s, kz_r, ec_s, ec_r, ex_s, ex_r,
@@ -72,7 +72,6 @@
     chunks = width // chunk
     k_rows = width // count
     e_rows = width // 4
-    group = 4
 
     core_peer = {"cross": 1 - core}
     x_peer = {"slab": slab + 1 - 2 * x}
@@ -91,6 +90,7 @@
         pltpu.make_async_copy(basis, ext.at[pl.ds(layer, rows)], load_sem.at[0]),
         pltpu.make_async_copy(stiff, stiff_v, load_sem.at[1]),
         pltpu.make_async_copy(soft, soft_v, load_sem.at[2]),
+        pltpu.make_async_copy(under, mask_v, load_sem.at[3]),
     ]
     for load in loads:
         load.start()
@@ -125,75 +125,53 @@
         last_out.start()
         lower_out.start()
 
-    loads[0].wait()
-
-    def turn(g, _):
-        at = pl.multiple_of(g * chunk, chunk)
-        turned[:, pl.ds(at, chunk)] = ext[pl.ds(pl.multiple_of(layer + at, layer), chunk), :].T
-        return 0
-
-    lax.fori_loop(0, rows // chunk, turn, 0)
-    loads[1].wait()
-    loads[2].wait()
-
-    @pl.when(here > 0)
-    def _():
-        last_out.wait_recv()
-        lower_out.wait_recv()
-
-    @pl.when(here == 0)
-    def _():
-        ext[pl.ds(0, layer), :] = jnp.zeros((layer, width), BF16)
-        stiff_p[...] = jnp.zeros(stiff_p.shape, BF16)
-
-    @pl.when(here < count - 1)
-    def _():
-        first_out.wait_recv()
-
-    @pl.when(here == count - 1)
-    def _():
-        ext[pl.ds(layer + rows, layer), :] = jnp.zeros((layer, width), BF16)
+    for load in loads:
+        load.wait()
+
+    def halo_in():
+        @pl.when(here > 0)
+        def _():
+            last_out.wait_recv()
+            lower_out.wait_recv()
+
+        @pl.when(here == 0)
+        def _():
+            ext[pl.ds(0, layer), :] = jnp.zeros((layer, width), BF16)
+            stiff_p[...] = jnp.zeros(stiff_p.shape, BF16)
+
+        @pl.when(here < count - 1)
+        def _():
+            first_out.wait_recv()
+
+        @pl.when(here == count - 1)
+        def _():
+            ext[pl.ds(layer + rows, layer), :] = jnp.zeros((layer, width), BF16)
 
     def stiff_chunk(j):
         cols = pl.ds(j * chunk, chunk)
-
-        def step(g, carry):
-            for i in range(group):
-                c = g * group + i
-                at = pl.multiple_of(c * layer, layer)
-                prod = jnp.dot(
-                    stiff_v[c],
-                    ext[pl.ds(pl.multiple_of(at + layer, layer), 2 * layer), cols],
-                    preferred_element_type=F32,
-                )
-                acted[pl.ds(at, layer), cols] = (prod[:layer] + carry).astype(BF16)
-                carry = prod[layer:]
-            return carry
-
         carry = jnp.dot(stiff_p[...], ext[pl.ds(0, 2 * layer), cols], preferred_element_type=F32)
-        lax.fori_loop(0, cells // group, step, carry)
+        for c in range(cells):
+            at = c * layer
+            prod = jnp.dot(
+                stiff_v[c], ext[pl.ds(at + layer, 2 * layer), cols], preferred_element_type=F32
+            )
+            acted[pl.ds(at, layer), cols] = (prod[:layer] + carry).astype(BF16)
+            carry = prod[layer:]
 
     def soft_chunk(j):
         cols = pl.ds(j * chunk, chunk)
-
-        def step(g, _):
-            for i in range(group):
-                c = g * group + i
-                at = pl.multiple_of(c * layer, layer)
-                masked = soft_v[c] * under[c].astype(F32).astype(BF16)
-                prod = jnp.dot(
-                    masked,
-                    ext[pl.ds(pl.multiple_of(at + layer, layer), layer), cols],
-                    preferred_element_type=F32,
-                )
-                acted[pl.ds(at, layer), cols] = prod.astype(BF16)
-            return 0
-
-        lax.fori_loop(0, cells // group, step, 0)
-
-    def project(j):
-        return jnp.dot(
-            turned[...], acted[:, pl.ds(j * chunk, chunk)], preferred_element_type=F32
+        for c in range(cells):
+            at = c * layer
+            masked = soft_v[c] * mask_v[c].astype(F32).astype(BF16)
+            prod = jnp.dot(
+                masked, ext[pl.ds(at + layer, layer), cols], preferred_element_type=F32
+            )
+            softened[pl.ds(at, layer), cols] = prod.astype(BF16)
+
+    def project(right, j):
+        return lax.dot_general(
+            ext[pl.ds(layer, rows), :], right[:, pl.ds(j * chunk, chunk)],
+            (((0,), (0,)), ((), ())), preferred_element_type=F32,
         )
 
     kc = [remote(k_core_s.at[j, 1 - core], k_core_r.at[j], kc_s.at[j], kc_r.at[j], core_peer)
@@ -206,7 +184,7 @@
     ex = [remote(e_x_s.at[j], e_x_r.at[j], ex_s.at[j], ex_r.at[j], x_peer) for j in range(chunks)]
 
     def k_start(j):
-        part = project(j)
+        part = project(acted, j)
         for c in range(2):
             for xx in range(2):
                 for zz in range(nz):
@@ -237,7 +215,7 @@
         k_out[:, pl.ds(j * chunk, chunk)] = total
 
     def e_start(j):
-        part = project(j)
+        part = project(softened, j)
         for c in range(2):
             for xx in range(2):
                 at = (xx * 2 + c) * e_rows
@@ -259,22 +237,23 @@
     def ex_in(j):
         return e_x_r[j].astype(F32)
 
+    soft_chunk(0)
+    e_start(0)
+    halo_in()
     stiff_chunk(0)
     k_start(0)
+    e_across(0)
     stiff_chunk(1)
     k_across(0)
     k_start(1)
-    soft_chunk(0)
+    soft_chunk(1)
     k_across(1)
+    e_start(1)
     k_along(0)
-    e_start(0)
-    soft_chunk(1)
-    e_across(0)
+    e_end(0)
+    e_across(1)
     k_along(1)
-    e_start(1)
     k_end(0)
-    e_across(1)
-    e_end(0)
     k_end(1)
     e_end(1)
 
@@ -304,7 +283,7 @@
     chunks = width // chunk
     k_rows = width // (4 * nz)
     e_rows = width // 4
-    hbm = pl.BlockSpec(memory_space=pl.ANY)
+    hbm = pl.BlockSpec(memory_space=pltpu.HBM)
     vmem = pl.BlockSpec(memory_space=pltpu.VMEM)
     dma = pltpu.SemaphoreType.DMA
     return pl.pallas_call(
@@ -313,14 +292,15 @@
             jax.ShapeDtypeStruct((k_rows, width), F32),
             jax.ShapeDtypeStruct((e_rows, width), F32),
         ),
-        in_specs=[hbm, hbm, hbm, pl.BlockSpec(memory_space=pltpu.SMEM)],
+        in_specs=[hbm] * 4,
         out_specs=(vmem, vmem),
         scratch_shapes=[
             pltpu.VMEM((rows + 2 * layer, width), BF16),
-            pltpu.VMEM((width, rows), BF16),
             pltpu.VMEM((cells, 2 * layer, 2 * layer), BF16),
             pltpu.VMEM((layer, 2 * layer), BF16),
             pltpu.VMEM((cells, layer, layer), BF16),
+            pltpu.SMEM((cells,), jnp.int32),
+            pltpu.VMEM((rows, width), BF16),
             pltpu.VMEM((rows, width), BF16),
             pltpu.VMEM((chunks, 2, 2, nz, k_rows, chunk), F32),
             pltpu.VMEM((chunks, 2, 2, nz, k_rows, chunk), BF16),
@@ -334,13 +314,13 @@
             pltpu.VMEM((chunks, 2, e_rows, chunk), BF16),
             pltpu.VMEM((chunks, e_rows, chunk), BF16),
             pltpu.VMEM((chunks, e_rows, chunk), BF16),
-            dma((3,)), dma((3,)), dma((3,)),
+            dma((4,)), dma((3,)), dma((3,)),
             dma((chunks,)), dma((chunks,)), dma((chunks,)), dma((chunks,)),
             dma((chunks, nz - 1)), dma((chunks, nz - 1)),
             dma((chunks,)), dma((chunks,)), dma((chunks,)), dma((chunks,)),
         ],
         compiler_params=pltpu.CompilerParams(
-            collective_id=0, has_side_effects=True, vmem_limit_bytes=48 << 20
+            collective_id=0, has_side_effects=True, vmem_limit_bytes=60 << 20
         ),
         name="fused",
     )(basis.reshape(rows, width), stiff, soft, under)

time: 31.6 us -> 25.3 us (0.80)
  Pallas kernels: 24.8 us -> 21.3 us
  local copies, waits for them, and re-layouts: 5.84 us -> 3.14 us
    pallas_call x1, Pallas kernels: 24.8 us -> 21.3 us  [fused_body(): pl.pallas_call(functools.partial(fused_kernel, nz, cells, layer, width, c...]
    unnamed x10 -> x2, local copies, waits for them, and re-layouts: 5.84 us -> 3.14 us
where the time goes in v2:
time: 25.3 us; the launch traced here: 25.1 us
  Pallas kernels  21.3 us (84%)
  local copies, waits for them, and re-layouts  3.14 us (12%)
  between operations  0.64 us (3%)
    pallas_call x1, Pallas kernels, fused_body(): pl.pallas_call(functools.partial(fused_kernel, nz, cells, layer, width, c...  21.3 us
    unnamed x2, local copies, waits for them, and re-layouts  3.14 us

profile of v2, /device:TPU:0, one launch (start us, length us, event | category | flops | bytes accessed | tf_op | source)
XLA Modules:
  0.0 25.1 jit_solution(5590846904443218491)
XLA Ops:
  0.6 21.3 %fused.1 = (f32[32,512]{1,0:T(8,128)}, f32[128,512]{1,0:T(8,128)}) custom-call(bf16[2048,512]{1,0:T(8,128)(2,1)} %bitcast.1, bf16[32,128,128]{2,1,0:T(8,128)(2,1)} %stiff.1, bf16[32,64,64]{2,1,0:T(8,128)(2,1)} %soft.1, s32[32]{0:T(128)} %under.1), custom_call_target="tpu_custom_call" | custom-call | tf_op jit(solution)/shard_map/fused/pallas_call | solution.py:289
  21.9 1.5 %copy.8 = f32[32,512]{1,0:T(8,128)} copy(f32[32,512]{1,0:T(8,128)} %get-tuple-element.4) | data formatting | bytes 131072
  23.4 1.7 %copy.9 = f32[128,512]{1,0:T(8,128)} copy(f32[128,512]{1,0:T(8,128)} %get-tuple-element.5) | data formatting | bytes 524288

commit v3 on v2

--- a/solution.py
+++ b/solution.py
@@ -58,10 +58,10 @@
 def fused_kernel(
     nz, cells, layer, width, chunk,
     basis, stiff, soft, under, k_out, e_out,
-    ext, stiff_v, stiff_p, soft_v, mask_v, acted, softened,
-    k_own, k_core_s, k_core_r, k_x_s, k_x_r, k_z_s, k_z_r,
-    e_own, e_core_s, e_core_r, e_x_s, e_x_r,
-    load_sem, halo_s, halo_r, kc_s, kc_r, kx_s, kx_r, kz_s, kz_r, ec_s, ec_r, ex_s, ex_r,
+    ext, stiff_v, stiff_p, soft_v, mask_v, acted, softened, held,
+    k_own, k_core_s, k_core_r, k_s, k_r, k_res,
+    e_own, e_core_s, e_core_r, e_x_s, e_x_r, e_res,
+    load_sem, halo_s, halo_r, kc_s, kc_r, kp_s, kp_r, ec_s, ec_r, ex_s, ex_r, ko_sem, eo_sem,
 ):
     slab = lax.axis_index("slab")
     core = lax.axis_index("cross")
@@ -75,27 +75,27 @@
 
     core_peer = {"cross": 1 - core}
     x_peer = {"slab": slab + 1 - 2 * x}
-    z_peers = [{"slab": ((z + d) % nz) * 2 + x} for d in range(1, nz)]
+    turns = [nz // 2] + [d for d in range(1, nz) if d != nz // 2]
+    places = [((z + d) % nz, (x + e) % 2) for d in turns for e in (1, 0)] + [(z, 1 - x)]
+    chip_peers = [{"slab": zz * 2 + xx} for zz, xx in places]
     before = (here + count - 1) % count
     after = (here + 1) % count
     before_peer = {"slab": before // 2, "cross": before % 2}
     after_peer = {"slab": after // 2, "cross": after % 2}
 
     barrier = pltpu.get_barrier_semaphore()
-    peers = [core_peer, x_peer, *z_peers, before_peer, after_peer]
+    peers = [*chip_peers, core_peer, before_peer, after_peer]
     for peer in peers:
         pl.semaphore_signal(barrier, inc=1, device_id=peer, device_id_type=MESH)
 
     loads = [
+        pltpu.make_async_copy(under, mask_v, load_sem.at[3]),
+        pltpu.make_async_copy(soft, soft_v, load_sem.at[2]),
         pltpu.make_async_copy(basis, ext.at[pl.ds(layer, rows)], load_sem.at[0]),
         pltpu.make_async_copy(stiff, stiff_v, load_sem.at[1]),
-        pltpu.make_async_copy(soft, soft_v, load_sem.at[2]),
-        pltpu.make_async_copy(under, mask_v, load_sem.at[3]),
     ]
     for load in loads:
         load.start()
-
-    pl.semaphore_wait(barrier, len(peers))
 
     def remote(src, dst, send, recv, peer):
         return pltpu.make_async_remote_copy(
@@ -116,17 +116,15 @@
         halo_s.at[2], halo_r.at[2], after_peer,
     )
 
-    @pl.when(here > 0)
-    def _():
-        first_out.start()
-
-    @pl.when(here < count - 1)
-    def _():
-        last_out.start()
-        lower_out.start()
-
-    for load in loads:
-        load.wait()
+    def halo_out():
+        @pl.when(here > 0)
+        def _():
+            first_out.start()
+
+        @pl.when(here < count - 1)
+        def _():
+            last_out.start()
+            lower_out.start()
 
     def halo_in():
         @pl.when(here > 0)
@@ -147,16 +145,25 @@
         def _():
             ext[pl.ds(layer + rows, layer), :] = jnp.zeros((layer, width), BF16)
 
-    def stiff_chunk(j):
+    def across(left, right):
+        return lax.dot_general(
+            left, right, (((0,), (0,)), ((), ())), preferred_element_type=F32
+        )
+
+    def stiff_inner(j):
         cols = pl.ds(j * chunk, chunk)
-        carry = jnp.dot(stiff_p[...], ext[pl.ds(0, 2 * layer), cols], preferred_element_type=F32)
-        for c in range(cells):
+        carry = None
+        for c in range(cells - 1):
             at = c * layer
             prod = jnp.dot(
                 stiff_v[c], ext[pl.ds(at + layer, 2 * layer), cols], preferred_element_type=F32
             )
-            acted[pl.ds(at, layer), cols] = (prod[:layer] + carry).astype(BF16)
+            if c == 0:
+                held[0, :, cols] = prod[:layer]
+            else:
+                acted[pl.ds(at, layer), cols] = (prod[:layer] + carry).astype(BF16)
             carry = prod[layer:]
+        held[1, :, cols] = carry
 
     def soft_chunk(j):
         cols = pl.ds(j * chunk, chunk)
@@ -168,61 +175,73 @@
             )
             softened[pl.ds(at, layer), cols] = prod.astype(BF16)
 
-    def project(right, j):
-        return lax.dot_general(
-            ext[pl.ds(layer, rows), :], right[:, pl.ds(j * chunk, chunk)],
-            (((0,), (0,)), ((), ())), preferred_element_type=F32,
-        )
-
     kc = [remote(k_core_s.at[j, 1 - core], k_core_r.at[j], kc_s.at[j], kc_r.at[j], core_peer)
           for j in range(chunks)]
-    kx = [remote(k_x_s.at[j], k_x_r.at[j], kx_s.at[j], kx_r.at[j], x_peer) for j in range(chunks)]
-    kz = [[remote(k_z_s.at[j, d], k_z_r.at[j, d], kz_s.at[j, d], kz_r.at[j, d], z_peers[d])
-           for d in range(nz - 1)] for j in range(chunks)]
+    kp = [[remote(k_s.at[j, p], k_r.at[j, p], kp_s.at[j, p], kp_r.at[j, p], peer)
+           for p, peer in enumerate(chip_peers)] for j in range(chunks)]
     ec = [remote(e_core_s.at[j, 1 - core], e_core_r.at[j], ec_s.at[j], ec_r.at[j], core_peer)
           for j in range(chunks)]
     ex = [remote(e_x_s.at[j], e_x_r.at[j], ex_s.at[j], ex_r.at[j], x_peer) for j in range(chunks)]
-
-    def k_start(j):
-        part = project(acted, j)
+    ko = [pltpu.make_async_copy(k_res.at[j], k_out.at[:, pl.ds(j * chunk, chunk)], ko_sem.at[j])
+          for j in range(chunks)]
+    eo = [pltpu.make_async_copy(e_res.at[j], e_out.at[:, pl.ds(j * chunk, chunk)], eo_sem.at[j])
+          for j in range(chunks)]
+
+    def k_blocks():
         for c in range(2):
             for xx in range(2):
                 for zz in range(nz):
-                    at = ((zz * 2 + xx) * 2 + c) * k_rows
-                    block = part[at:at + k_rows]
-                    k_own[j, c, xx, zz] = block
-                    k_core_s[j, c, xx, zz] = block.astype(BF16)
+                    yield c, xx, zz, ((zz * 2 + xx) * 2 + c) * k_rows
+
+    def k_inner(j):
+        part = across(
+            ext[pl.ds(2 * layer, rows - 2 * layer), :],
+            acted[pl.ds(layer, rows - 2 * layer), pl.ds(j * chunk, chunk)],
+        )
+        for c, xx, zz, at in k_blocks():
+            k_own[j, c, xx, zz] = part[at:at + k_rows]
+
+    def k_start(j):
+        cols = pl.ds(j * chunk, chunk)
+        low = held[0, :, cols] + jnp.dot(
+            stiff_p[...], ext[pl.ds(0, 2 * layer), cols], preferred_element_type=F32
+        )
+        high = held[1, :, cols] + jnp.dot(
+            stiff_v[cells - 1, pl.ds(0, layer)], ext[pl.ds(rows, 2 * layer), cols],
+            preferred_element_type=F32,
+        )
+        part = across(
+            jnp.concatenate([ext[pl.ds(layer, layer), :], ext[pl.ds(rows, layer), :]], axis=0),
+            jnp.concatenate([low.astype(BF16), high.astype(BF16)], axis=0),
+        )
+        for c, xx, zz, at in k_blocks():
+            block = k_own[j, c, xx, zz] + part[at:at + k_rows]
+            k_own[j, c, xx, zz] = block
+            k_core_s[j, c, xx, zz] = block.astype(BF16)
         kc[j].start()
 
     def k_across(j):
         kc[j].wait_recv()
-        k_x_s[j] = (k_own[j, core, 1 - x] + k_core_r[j, 1 - x].astype(F32)).astype(BF16)
-        kx[j].start()
-        k_own[j, core, x] = k_own[j, core, x] + k_core_r[j, x].astype(F32)
-
-    def k_along(j):
-        kx[j].wait_recv()
-        for d in range(nz - 1):
-            to = (z + d + 1) % nz
-            k_z_s[j, d] = (k_own[j, core, x, to] + k_x_r[j, to].astype(F32)).astype(BF16)
-            kz[j][d].start()
+        for p, (zz, xx) in enumerate(places):
+            k_s[j, p] = (k_own[j, core, xx, zz] + k_core_r[j, xx, zz].astype(F32)).astype(BF16)
+            kp[j][p].start()
 
     def k_end(j):
-        total = k_own[j, core, x, z] + k_x_r[j, z].astype(F32)
-        for d in range(nz - 1):
-            kz[j][d].wait_recv()
-            total = total + k_z_r[j, d].astype(F32)
-        k_out[:, pl.ds(j * chunk, chunk)] = total
-
-    def e_start(j):
-        part = project(softened, j)
+        total = k_own[j, core, x, z] + k_core_r[j, x, z].astype(F32)
+        for p in reversed(range(len(places))):
+            kp[j][p].wait_recv()
+            total = total + k_r[j, p].astype(F32)
+        k_res[j] = total
+        ko[j].start()
+
+    def e_inner(j):
+        part = across(ext[pl.ds(layer, rows), :], softened[:, pl.ds(j * chunk, chunk)])
         for c in range(2):
             for xx in range(2):
                 at = (xx * 2 + c) * e_rows
                 block = part[at:at + e_rows]
                 e_own[j, c, xx] = block
                 e_core_s[j, c, xx] = block.astype(BF16)
-        ec[j].start()
 
     def e_across(j):
         ec[j].wait_recv()
@@ -232,30 +251,35 @@
     def e_end(j):
         mine = e_own[j, core, x] + e_core_r[j, x].astype(F32)
         ex[j].wait_recv()
-        e_out[:, pl.ds(j * chunk, chunk)] = mine + ex_in(j)
-
-    def ex_in(j):
-        return e_x_r[j].astype(F32)
-
+        e_res[j] = mine + e_x_r[j].astype(F32)
+        eo[j].start()
+
+    for load in loads[:3]:
+        load.wait()
     soft_chunk(0)
-    e_start(0)
+    e_inner(0)
+    pl.semaphore_wait(barrier, len(peers))
+    halo_out()
+    ec[0].start()
+    loads[3].wait()
+    stiff_inner(0)
+    k_inner(0)
+    e_across(0)
+    stiff_inner(1)
+    k_inner(1)
+    soft_chunk(1)
     halo_in()
-    stiff_chunk(0)
     k_start(0)
-    e_across(0)
-    stiff_chunk(1)
+    k_start(1)
+    e_inner(1)
+    ec[1].start()
     k_across(0)
-    k_start(1)
-    soft_chunk(1)
     k_across(1)
-    e_start(1)
-    k_along(0)
+    e_across(1)
     e_end(0)
-    e_across(1)
-    k_along(1)
+    e_end(1)
     k_end(0)
     k_end(1)
-    e_end(1)
 
     @pl.when(here > 0)
     def _():
@@ -268,11 +292,30 @@
 
     for j in range(chunks):
         kc[j].wait_send()
-        kx[j].wait_send()
-        for d in range(nz - 1):
-            kz[j][d].wait_send()
+        for copy in kp[j]:
+            copy.wait_send()
         ec[j].wait_send()
         ex[j].wait_send()
+        eo[j].wait()
+        ko[j].wait()
+
+
+def hand_on(k_in, e_in, k_out, e_out, k_v, e_v, sem):
+    parts = 2
+    size = e_v.shape[0] // parts
+    reads = [pltpu.make_async_copy(e_in.at[pl.ds(i * size, size)], e_v.at[pl.ds(i * size, size)],
+                                   sem.at[0, i]) for i in range(parts)]
+    writes = [pltpu.make_async_copy(e_v.at[pl.ds(i * size, size)], e_out.at[pl.ds(i * size, size)],
+                                    sem.at[1, i]) for i in range(parts)]
+    reads.append(pltpu.make_async_copy(k_in, k_v, sem.at[0, parts]))
+    writes.append(pltpu.make_async_copy(k_v, k_out, sem.at[1, parts]))
+    for copy in reads:
+        copy.start()
+    for read, write in zip(reads, writes):
+        read.wait()
+        write.start()
+    for copy in writes:
+        copy.wait()
 
 
 def fused_body(basis, stiff, soft, under):
@@ -283,17 +326,18 @@
     chunks = width // chunk
     k_rows = width // (4 * nz)
     e_rows = width // 4
-    hbm = pl.BlockSpec(memory_space=pltpu.HBM)
-    vmem = pl.BlockSpec(memory_space=pltpu.VMEM)
+    others = 2 * nz - 1
+    hbm = pl.BlockSpec(memory_space=pl.ANY)
     dma = pltpu.SemaphoreType.DMA
-    return pl.pallas_call(
+    shapes = (
+        jax.ShapeDtypeStruct((k_rows, width), F32),
+        jax.ShapeDtypeStruct((e_rows, width), F32),
+    )
+    k_red, e_red = pl.pallas_call(
         functools.partial(fused_kernel, nz, cells, layer, width, chunk),
-        out_shape=(
-            jax.ShapeDtypeStruct((k_rows, width), F32),
-            jax.ShapeDtypeStruct((e_rows, width), F32),
-        ),
+        out_shape=shapes,
         in_specs=[hbm] * 4,
-        out_specs=(vmem, vmem),
+        out_specs=(hbm, hbm),
         scratch_shapes=[
             pltpu.VMEM((rows + 2 * layer, width), BF16),
             pltpu.VMEM((cells, 2 * layer, 2 * layer), BF16),
@@ -302,28 +346,41 @@
             pltpu.SMEM((cells,), jnp.int32),
             pltpu.VMEM((rows, width), BF16),
             pltpu.VMEM((rows, width), BF16),
+            pltpu.VMEM((2, layer, width), F32),
             pltpu.VMEM((chunks, 2, 2, nz, k_rows, chunk), F32),
             pltpu.VMEM((chunks, 2, 2, nz, k_rows, chunk), BF16),
             pltpu.VMEM((chunks, 2, nz, k_rows, chunk), BF16),
-            pltpu.VMEM((chunks, nz, k_rows, chunk), BF16),
-            pltpu.VMEM((chunks, nz, k_rows, chunk), BF16),
-            pltpu.VMEM((chunks, nz - 1, k_rows, chunk), BF16),
-            pltpu.VMEM((chunks, nz - 1, k_rows, chunk), BF16),
+            pltpu.VMEM((chunks, others, k_rows, chunk), BF16),
+            pltpu.VMEM((chunks, others, k_rows, chunk), BF16),
+            pltpu.VMEM((chunks, k_rows, chunk), F32),
             pltpu.VMEM((chunks, 2, 2, e_rows, chunk), F32),
             pltpu.VMEM((chunks, 2, 2, e_rows, chunk), BF16),
             pltpu.VMEM((chunks, 2, e_rows, chunk), BF16),
             pltpu.VMEM((chunks, e_rows, chunk), BF16),
             pltpu.VMEM((chunks, e_rows, chunk), BF16),
+            pltpu.VMEM((chunks, e_rows, chunk), F32),
             dma((4,)), dma((3,)), dma((3,)),
+            dma((chunks,)), dma((chunks,)),
+            dma((chunks, others)), dma((chunks, others)),
             dma((chunks,)), dma((chunks,)), dma((chunks,)), dma((chunks,)),
-            dma((chunks, nz - 1)), dma((chunks, nz - 1)),
-            dma((chunks,)), dma((chunks,)), dma((chunks,)), dma((chunks,)),
+            dma((chunks,)), dma((chunks,)),
         ],
         compiler_params=pltpu.CompilerParams(
             collective_id=0, has_side_effects=True, vmem_limit_bytes=60 << 20
         ),
         name="fused",
     )(basis.reshape(rows, width), stiff, soft, under)
+    return pl.pallas_call(
+        hand_on,
+        out_shape=shapes,
+        in_specs=[hbm, hbm],
+        out_specs=(hbm, hbm),
+        scratch_shapes=[
+            pltpu.VMEM(shapes[0].shape, F32), pltpu.VMEM(shapes[1].shape, F32), dma((2, 3)),
+        ],
+        compiler_params=pltpu.CompilerParams(vmem_limit_bytes=60 << 20),
+        name="hand_on",
+    )(k_red, e_red)
 
 
 def solution(mesh):

time: 25.3 us -> 23.8 us (0.941)
  local copies, waits for them, and re-layouts: 3.14 us -> 0 us
  Pallas kernels: 21.3 us -> 23 us
    unnamed x2 -> x0, local copies, waits for them, and re-layouts: 3.14 us -> none
    pallas_call x0 -> x1, Pallas kernels: none -> 1.69 us  [fused_body(): pl.pallas_call(hand_on, out_shape=shapes, in_specs=[hbm, hbm], out_specs=...]
where the time goes in v3:
time: 23.8 us; the launch traced here: 23.6 us
  Pallas kernels  23 us (97%)
  between operations  0.64 us (3%)
    pallas_call x1, Pallas kernels, fused_body(): pl.pallas_call(functools.partial(fused_kernel, nz, cells, layer, width, c...  21.3 us
    pallas_call x1, Pallas kernels, fused_body(): pl.pallas_call(hand_on, out_shape=shapes, in_specs=[hbm, hbm], out_specs=...  1.69 us

profile of v3, /device:TPU:0, one launch (start us, length us, event | category | flops | bytes accessed | tf_op | source)
XLA Modules:
  0.0 23.6 jit_solution(7337487183380878159)
XLA Ops:
  0.6 21.3 %fused.1 = (f32[32,512]{1,0:T(8,128)}, f32[128,512]{1,0:T(8,128)}) custom-call(bf16[2048,512]{1,0:T(8,128)(2,1)} %bitcast.1, bf16[32,128,128]{2,1,0:T(8,128)(2,1)} %stiff.1, bf16[32,64,64]{2,1,0:T(8,128)(2,1)} %soft.1, s32[32]{0:T(128)} %under.1), custom_call_target="tpu_custom_call" | custom-call | tf_op jit(solution)/shard_map/fused/pallas_call | solution.py:336
  21.9 1.7 %hand_on.1 = (f32[32,512]{1,0:T(8,128)}, f32[128,512]{1,0:T(8,128)}) custom-call(f32[32,512]{1,0:T(8,128)} %get-tuple-element.4.k_in, f32[128,512]{1,0:T(8,128)} %get-tuple-element.5.e_in), custom_call_target="tpu_custom_call" | custom-call | tf_op jit(solution)/shard_map/hand_on/pallas_call | solution.py:373

commit v4 on v3

--- a/solution.py
+++ b/solution.py
@@ -59,9 +59,9 @@
     nz, cells, layer, width, chunk,
     basis, stiff, soft, under, k_out, e_out,
     ext, stiff_v, stiff_p, soft_v, mask_v, acted, softened, held,
-    k_own, k_core_s, k_core_r, k_s, k_r, k_res,
-    e_own, e_core_s, e_core_r, e_x_s, e_x_r, e_res,
-    load_sem, halo_s, halo_r, kc_s, kc_r, kp_s, kp_r, ec_s, ec_r, ex_s, ex_r, ko_sem, eo_sem,
+    k_own, k_core_s, k_core_r, k_s, k_r,
+    e_own, e_core_s, e_core_r, e_x_s, e_x_r,
+    load_sem, halo_s, halo_r, kc_s, kc_r, kp_s, kp_r, ec_s, ec_r, ex_s, ex_r,
 ):
     slab = lax.axis_index("slab")
     core = lax.axis_index("cross")
@@ -182,10 +182,6 @@
     ec = [remote(e_core_s.at[j, 1 - core], e_core_r.at[j], ec_s.at[j], ec_r.at[j], core_peer)
           for j in range(chunks)]
     ex = [remote(e_x_s.at[j], e_x_r.at[j], ex_s.at[j], ex_r.at[j], x_peer) for j in range(chunks)]
-    ko = [pltpu.make_async_copy(k_res.at[j], k_out.at[:, pl.ds(j * chunk, chunk)], ko_sem.at[j])
-          for j in range(chunks)]
-    eo = [pltpu.make_async_copy(e_res.at[j], e_out.at[:, pl.ds(j * chunk, chunk)], eo_sem.at[j])
-          for j in range(chunks)]
 
     def k_blocks():
         for c in range(2):
@@ -231,8 +227,7 @@
         for p in reversed(range(len(places))):
             kp[j][p].wait_recv()
             total = total + k_r[j, p].astype(F32)
-        k_res[j] = total
-        ko[j].start()
+        k_out[:, pl.ds(j * chunk, chunk)] = total
 
     def e_inner(j):
         part = across(ext[pl.ds(layer, rows), :], softened[:, pl.ds(j * chunk, chunk)])
@@ -251,8 +246,7 @@
     def e_end(j):
         mine = e_own[j, core, x] + e_core_r[j, x].astype(F32)
         ex[j].wait_recv()
-        e_res[j] = mine + e_x_r[j].astype(F32)
-        eo[j].start()
+        e_out[:, pl.ds(j * chunk, chunk)] = mine + e_x_r[j].astype(F32)
 
     for load in loads[:3]:
         load.wait()
@@ -296,25 +290,16 @@
             copy.wait_send()
         ec[j].wait_send()
         ex[j].wait_send()
-        eo[j].wait()
-        ko[j].wait()
-
-
-def hand_on(k_in, e_in, k_out, e_out, k_v, e_v, sem):
-    parts = 2
-    size = e_v.shape[0] // parts
-    reads = [pltpu.make_async_copy(e_in.at[pl.ds(i * size, size)], e_v.at[pl.ds(i * size, size)],
-                                   sem.at[0, i]) for i in range(parts)]
-    writes = [pltpu.make_async_copy(e_v.at[pl.ds(i * size, size)], e_out.at[pl.ds(i * size, size)],
-                                    sem.at[1, i]) for i in range(parts)]
-    reads.append(pltpu.make_async_copy(k_in, k_v, sem.at[0, parts]))
-    writes.append(pltpu.make_async_copy(k_v, k_out, sem.at[1, parts]))
-    for copy in reads:
+
+
+def hand_on(k_in, e_in, k_out, e_out, sem):
+    copies = [
+        pltpu.make_async_copy(e_in, e_out, sem.at[0]),
+        pltpu.make_async_copy(k_in, k_out, sem.at[1]),
+    ]
+    for copy in copies:
         copy.start()
-    for read, write in zip(reads, writes):
-        read.wait()
-        write.start()
-    for copy in writes:
+    for copy in copies:
         copy.wait()
 
 
@@ -328,6 +313,7 @@
     e_rows = width // 4
     others = 2 * nz - 1
     hbm = pl.BlockSpec(memory_space=pl.ANY)
+    vmem = pl.BlockSpec(memory_space=pltpu.VMEM)
     dma = pltpu.SemaphoreType.DMA
     shapes = (
         jax.ShapeDtypeStruct((k_rows, width), F32),
@@ -335,9 +321,9 @@
     )
     k_red, e_red = pl.pallas_call(
         functools.partial(fused_kernel, nz, cells, layer, width, chunk),
-        out_shape=shapes,
+        out_shape=(pltpu.VMEM((k_rows, width), F32), pltpu.VMEM((e_rows, width), F32)),
         in_specs=[hbm] * 4,
-        out_specs=(hbm, hbm),
+        out_specs=(vmem, vmem),
         scratch_shapes=[
             pltpu.VMEM((rows + 2 * layer, width), BF16),
             pltpu.VMEM((cells, 2 * layer, 2 * layer), BF16),
@@ -352,18 +338,15 @@
             pltpu.VMEM((chunks, 2, nz, k_rows, chunk), BF16),
             pltpu.VMEM((chunks, others, k_rows, chunk), BF16),
             pltpu.VMEM((chunks, others, k_rows, chunk), BF16),
-            pltpu.VMEM((chunks, k_rows, chunk), F32),
             pltpu.VMEM((chunks, 2, 2, e_rows, chunk), F32),
             pltpu.VMEM((chunks, 2, 2, e_rows, chunk), BF16),
             pltpu.VMEM((chunks, 2, e_rows, chunk), BF16),
             pltpu.VMEM((chunks, e_rows, chunk), BF16),
             pltpu.VMEM((chunks, e_rows, chunk), BF16),
-            pltpu.VMEM((chunks, e_rows, chunk), F32),
             dma((4,)), dma((3,)), dma((3,)),
             dma((chunks,)), dma((chunks,)),
             dma((chunks, others)), dma((chunks, others)),
             dma((chunks,)), dma((chunks,)), dma((chunks,)), dma((chunks,)),
-            dma((chunks,)), dma((chunks,)),
         ],
         compiler_params=pltpu.CompilerParams(
             collective_id=0, has_side_effects=True, vmem_limit_bytes=60 << 20
@@ -373,12 +356,10 @@
     return pl.pallas_call(
         hand_on,
         out_shape=shapes,
-        in_specs=[hbm, hbm],
+        in_specs=[vmem, vmem],
         out_specs=(hbm, hbm),
-        scratch_shapes=[
-            pltpu.VMEM(shapes[0].shape, F32), pltpu.VMEM(shapes[1].shape, F32), dma((2, 3)),
-        ],
-        compiler_params=pltpu.CompilerParams(vmem_limit_bytes=60 << 20),
+        scratch_shapes=[dma((2,))],
+        compiler_params=pltpu.CompilerParams(vmem_limit_bytes=32 << 20),
         name="hand_on",
     )(k_red, e_red)
 

time: 23.8 us -> 22.2 us (0.933)
  Pallas kernels: 23 us -> 21.4 us
    pallas_call x1, Pallas kernels: 1.69 us -> 0.73 us  [fused_body(): pl.pallas_call(hand_on, out_shape=shapes, in_specs=[vmem, vmem], out_spec...]
    pallas_call x1, Pallas kernels: 21.3 us -> 20.7 us  [fused_body(): pl.pallas_call(functools.partial(fused_kernel, nz, cells, layer, width, c...]
where the time goes in v4:
time: 22.2 us; the launch traced here: 22 us
  Pallas kernels  21.4 us (96%)
  between operations  0.64 us (3%)
    pallas_call x1, Pallas kernels, fused_body(): pl.pallas_call(functools.partial(fused_kernel, nz, cells, layer, width, c...  20.7 us
    pallas_call x1, Pallas kernels, fused_body(): pl.pallas_call(hand_on, out_shape=shapes, in_specs=[vmem, vmem], out_spec...  0.73 us

profile of v4, /device:TPU:0, one launch (start us, length us, event | category | flops | bytes accessed | tf_op | source)
XLA Modules:
  0.0 22.0 jit_solution(4324838411083689262)
XLA Ops:
  0.6 20.7 %fused.1 = (f32[32,512]{1,0:T(8,128)S(1)}, f32[128,512]{1,0:T(8,128)S(1)}) custom-call(bf16[2048,512]{1,0:T(8,128)(2,1)} %bitcast.1, bf16[32,128,128]{2,1,0:T(8,128)(2,1)} %stiff.1, bf16[32,64,64]{2,1,0:T(8,128)(2,1)} %soft.1, s32[32]{0:T(128)} %under.1), custom_call_target="tpu_custom_call" | custom-call | tf_op jit(solution)/shard_map/fused/pallas_call | solution.py:322
  21.3 0.7 %hand_on.1 = (f32[32,512]{1,0:T(8,128)}, f32[128,512]{1,0:T(8,128)}) custom-call(f32[32,512]{1,0:T(8,128)S(1)} %get-tuple-element.4.k_in, f32[128,512]{1,0:T(8,128)S(1)} %get-tuple-element.5.e_in), custom_call_target="tpu_custom_call" | custom-call | tf_op jit(solution)/shard_map/hand_on/pallas_call | solution.py:356

commit v5 on v4

--- a/solution.py
+++ b/solution.py
@@ -61,7 +61,7 @@
     ext, stiff_v, stiff_p, soft_v, mask_v, acted, softened, held,
     k_own, k_core_s, k_core_r, k_s, k_r,
     e_own, e_core_s, e_core_r, e_x_s, e_x_r,
-    load_sem, halo_s, halo_r, kc_s, kc_r, kp_s, kp_r, ec_s, ec_r, ex_s, ex_r,
+    load_sem, halo_s, halo_r, kc_s, kc_r, kp_s, kp_r, ec_s, ec_r, ex_s, ex_r, told,
 ):
     slab = lax.axis_index("slab")
     core = lax.axis_index("cross")
@@ -84,15 +84,51 @@
     after_peer = {"slab": after // 2, "cross": after % 2}
 
     barrier = pltpu.get_barrier_semaphore()
-    peers = [*chip_peers, core_peer, before_peer, after_peer]
-    for peer in peers:
+    for peer in (core_peer, x_peer):
         pl.semaphore_signal(barrier, inc=1, device_id=peer, device_id_type=MESH)
+    up_peer, down_peer = {"slab": slab + 2}, {"slab": slab - 2}
+    near = [
+        (here > 0, before_peer), (here < count - 1, after_peer),
+        (z > 0, down_peer), (z < nz - 1, up_peer),
+    ]
+    greeted = 2
+    for there, peer in near:
+        @pl.when(there)
+        def _():
+            pl.semaphore_signal(barrier, inc=1, device_id=peer, device_id_type=MESH)
+
+        greeted = greeted + there.astype(jnp.int32)
+
+    def tell(which, peer):
+        pl.semaphore_signal(told.at[which], inc=1, device_id=peer, device_id_type=MESH)
+
+    def tell_first():
+        if nz > 2:
+            pl.when(z == 1)(lambda: tell(0, up_peer))
+            pl.when(z == nz - 2)(lambda: tell(1, down_peer))
+
+    def tell_on():
+        @pl.when((z >= 2) & (z <= nz - 2))
+        def _():
+            pl.semaphore_wait(told.at[0], 1)
+            tell(0, up_peer)
+
+        @pl.when((z >= 1) & (z <= nz - 3))
+        def _():
+            pl.semaphore_wait(told.at[1], 1)
+            tell(1, down_peer)
+
+    def tell_last():
+        if nz > 2:
+            pl.when(z == nz - 1)(lambda: pl.semaphore_wait(told.at[0], 1))
+            pl.when(z == 0)(lambda: pl.semaphore_wait(told.at[1], 1))
+        tell(2, x_peer)
 
     loads = [
-        pltpu.make_async_copy(under, mask_v, load_sem.at[3]),
-        pltpu.make_async_copy(soft, soft_v, load_sem.at[2]),
         pltpu.make_async_copy(basis, ext.at[pl.ds(layer, rows)], load_sem.at[0]),
         pltpu.make_async_copy(stiff, stiff_v, load_sem.at[1]),
+        pltpu.make_async_copy(soft, soft_v, load_sem.at[2]),
+        pltpu.make_async_copy(under, mask_v, load_sem.at[3]),
     ]
     for load in loads:
         load.start()
@@ -248,27 +284,32 @@
         ex[j].wait_recv()
         e_out[:, pl.ds(j * chunk, chunk)] = mine + e_x_r[j].astype(F32)
 
-    for load in loads[:3]:
+    pl.semaphore_wait(barrier, greeted)
+    halo_out()
+    tell_first()
+    for load in loads[:2]:
         load.wait()
-    soft_chunk(0)
-    e_inner(0)
-    pl.semaphore_wait(barrier, len(peers))
-    halo_out()
-    ec[0].start()
-    loads[3].wait()
     stiff_inner(0)
     k_inner(0)
-    e_across(0)
+    tell_on()
     stiff_inner(1)
     k_inner(1)
-    soft_chunk(1)
+    tell_last()
     halo_in()
     k_start(0)
     k_start(1)
+    for load in loads[2:]:
+        load.wait()
+    soft_chunk(0)
+    pl.semaphore_wait(told.at[2], 1)
+    k_across(0)
+    k_across(1)
+    e_inner(0)
+    ec[0].start()
+    soft_chunk(1)
     e_inner(1)
     ec[1].start()
-    k_across(0)
-    k_across(1)
+    e_across(0)
     e_across(1)
     e_end(0)
     e_end(1)
@@ -347,6 +388,7 @@
             dma((chunks,)), dma((chunks,)),
             dma((chunks, others)), dma((chunks, others)),
             dma((chunks,)), dma((chunks,)), dma((chunks,)), dma((chunks,)),
+            pltpu.SemaphoreType.REGULAR((3,)),
         ],
         compiler_params=pltpu.CompilerParams(
             collective_id=0, has_side_effects=True, vmem_limit_bytes=60 << 20

time: 22.2 us -> 19.9 us (0.90)
  Pallas kernels: 21.4 us -> 19.1 us
    pallas_call x1, Pallas kernels: 20.7 us -> 18.3 us  [fused_body(): pl.pallas_call(functools.partial(fused_kernel, nz, cells, layer, width, c...]
where the time goes in v5:
time: 19.9 us; the launch traced here: 19.7 us
  Pallas kernels  19.1 us (96%)
  between operations  0.64 us (3%)
    pallas_call x1, Pallas kernels, fused_body(): pl.pallas_call(functools.partial(fused_kernel, nz, cells, layer, width, c...  18.3 us
    pallas_call x1, Pallas kernels, fused_body(): pl.pallas_call(hand_on, out_shape=shapes, in_specs=[vmem, vmem], out_spec...  0.73 us

profile of v5, /device:TPU:0, one launch (start us, length us, event | category | flops | bytes accessed | tf_op | source)
XLA Modules:
  0.0 19.7 jit_solution(16738234715322144991)
XLA Ops:
  0.6 18.3 %fused.1 = (f32[32,512]{1,0:T(8,128)S(1)}, f32[128,512]{1,0:T(8,128)S(1)}) custom-call(bf16[2048,512]{1,0:T(8,128)(2,1)} %bitcast.1, bf16[32,128,128]{2,1,0:T(8,128)(2,1)} %stiff.1, bf16[32,64,64]{2,1,0:T(8,128)(2,1)} %soft.1, s32[32]{0:T(128)} %under.1), custom_call_target="tpu_custom_call" | custom-call | tf_op jit(solution)/shard_map/fused/pallas_call | solution.py:363
  19.0 0.7 %hand_on.1 = (f32[32,512]{1,0:T(8,128)}, f32[128,512]{1,0:T(8,128)}) custom-call(f32[32,512]{1,0:T(8,128)S(1)} %get-tuple-element.4.k_in, f32[128,512]{1,0:T(8,128)S(1)} %get-tuple-element.5.e_in), custom_call_target="tpu_custom_call" | custom-call | tf_op jit(solution)/shard_map/hand_on/pallas_call | solution.py:398

commit v6 on v5

--- a/solution.py
+++ b/solution.py
@@ -76,7 +76,7 @@
     core_peer = {"cross": 1 - core}
     x_peer = {"slab": slab + 1 - 2 * x}
     turns = [nz // 2] + [d for d in range(1, nz) if d != nz // 2]
-    places = [((z + d) % nz, (x + e) % 2) for d in turns for e in (1, 0)] + [(z, 1 - x)]
+    places = [((z + d) % nz, (x + e) % 2) for e in (1, 0) for d in turns] + [(z, 1 - x)]
     chip_peers = [{"slab": zz * 2 + xx} for zz, xx in places]
     before = (here + count - 1) % count
     after = (here + 1) % count

time: 19.9 us -> 19.7 us (0.990)
  no operation moved by 1% of the time
where the time goes in v6:
time: 19.7 us; the launch traced here: 19.6 us
  Pallas kernels  19 us (96%)
  between operations  0.64 us (3%)
    pallas_call x1, Pallas kernels, fused_body(): pl.pallas_call(functools.partial(fused_kernel, nz, cells, layer, width, c...  18.2 us
    pallas_call x1, Pallas kernels, fused_body(): pl.pallas_call(hand_on, out_shape=shapes, in_specs=[vmem, vmem], out_spec...  0.73 us

profile of v6, /device:TPU:0, one launch (start us, length us, event | category | flops | bytes accessed | tf_op | source)
XLA Modules:
  0.0 19.6 jit_solution(10574257864983916657)
XLA Ops:
  0.6 18.2 %fused.1 = (f32[32,512]{1,0:T(8,128)S(1)}, f32[128,512]{1,0:T(8,128)S(1)}) custom-call(bf16[2048,512]{1,0:T(8,128)(2,1)} %bitcast.1, bf16[32,128,128]{2,1,0:T(8,128)(2,1)} %stiff.1, bf16[32,64,64]{2,1,0:T(8,128)(2,1)} %soft.1, s32[32]{0:T(128)} %under.1), custom_call_target="tpu_custom_call" | custom-call | tf_op jit(solution)/shard_map/fused/pallas_call | solution.py:363
  18.9 0.7 %hand_on.1 = (f32[32,512]{1,0:T(8,128)}, f32[128,512]{1,0:T(8,128)}) custom-call(f32[32,512]{1,0:T(8,128)S(1)} %get-tuple-element.4.k_in, f32[128,512]{1,0:T(8,128)S(1)} %get-tuple-element.5.e_in), custom_call_target="tpu_custom_call" | custom-call | tf_op jit(solution)/shard_map/hand_on/pallas_call | solution.py:398
